TPU v7x, 32 devices: a whole 2x2x4 slice. The times are simulated.
32 devices in a mesh: rep: 4 (over y, x), shard: 8 (over z, core).
Axes of the slice: x: 2, y: 2, z: 4, core: 2. Of those that a mesh axis runs over, the one named last changes fastest.
Arguments:
- local_dense: float32 [4, 1024, 1024], P('rep', 'shard'), may hold values from -6 to 6
- anchor_dense: float32 [1024, 1024], P('shard'), may hold values from -6 to 6
- momentum_dense: float32 [1024, 1024], P('shard'), may hold values from -6 to 6
- local_emb: float32 [4, 8192, 2048], P('rep', 'shard'), may hold values from -24 to 24
- anchor_emb: float32 [8192, 2048], P('shard'), may hold values from -24 to 24
- momentum_emb: float32 [8192, 2048], P('shard'), may hold values from -6 to 6
- proj_basis: float32 [2048, 64], P('shard'), may hold values from -6 to 6
Outputs:
- new_dense_anchor: float32 [1024, 1024], P('shard')
- new_dense_momentum: float32 [1024, 1024], P('shard')
- dense_weights: bfloat16 [1024, 1024], replicated
- new_emb_anchor: float32 [8192, 2048], P('shard')
- new_emb_momentum: float32 [8192, 2048], P('shard')
All inputs are finite; a program needn't handle non-finite values.
Results may differ from a plain program's by a relative error of at most 0.0004.
Values may be sent and summed in bfloat16 or wider, within the bound.
A program may use at most 128 MiB of HBM per device.

v0:
```python
import jax
import jax.numpy as jnp
from jax import lax
from jax.sharding import PartitionSpec as P

outer_rate = 0.7
momentum_rate = 0.9
highest = lax.Precision.HIGHEST


def dense_update(dense_sum, anchor_dense, momentum_dense, group_count):
    dense_grad = dense_sum / group_count
    dense_mom = momentum_rate * momentum_dense + dense_grad
    dense_new = anchor_dense - outer_rate * (dense_grad + momentum_rate * dense_mom)
    gathered = lax.all_gather(dense_new.astype(jnp.bfloat16), "shard", axis=0, tiled=True)
    return (dense_new, dense_mom, gathered)


def on_device(
    local_dense, anchor_dense, momentum_dense, local_emb, anchor_emb, momentum_emb, proj_basis
):
    group_count = lax.axis_size("rep")
    full_basis = lax.all_gather(proj_basis, "shard", axis=0, tiled=True)
    dense_diff = anchor_dense - local_dense[0]
    emb_diff = anchor_emb - local_emb[0]
    part_factor = jnp.dot(
        emb_diff, full_basis, precision=highest, preferred_element_type=jnp.float32
    )
    dense_sum, factor = lax.psum((dense_diff, part_factor), "rep")
    dense_new, dense_mom, gathered = dense_update(
        dense_sum, anchor_dense, momentum_dense, group_count
    )
    local_gram = lax.dot_general(
        factor,
        factor,
        (((0,), (0,)), ((), ())),
        precision=highest,
        preferred_element_type=jnp.float32,
    )
    gram_matrix = lax.psum(local_gram, "shard")
    chol_lower = jnp.linalg.cholesky(gram_matrix)
    ortho_rows = jax.scipy.linalg.solve_triangular(chol_lower, factor.T, lower=True).T
    coeff_share = lax.psum_scatter(
        lax.dot_general(
            emb_diff,
            ortho_rows,
            (((0,), (0,)), ((), ())),
            precision=highest,
            preferred_element_type=jnp.float32,
        ),
        "shard",
        scatter_dimension=0,
        tiled=True,
    )
    coeff_share = lax.psum(coeff_share, "rep")
    coefficients = lax.all_gather(coeff_share, "shard", axis=0, tiled=True)
    emb_grad = (
        lax.dot_general(
            ortho_rows,
            coefficients,
            (((1,), (1,)), ((), ())),
            precision=highest,
            preferred_element_type=jnp.float32,
        )
        / group_count
    )
    emb_mom = momentum_rate * momentum_emb + emb_grad
    emb_new = anchor_emb - outer_rate * (emb_grad + momentum_rate * emb_mom)
    return (dense_new, dense_mom, gathered, emb_new, emb_mom)


def solution(mesh):
    placed = (
        P("rep", "shard", None),
        P("shard", None),
        P("shard", None),
        P("rep", "shard", None),
        P("shard", None),
        P("shard", None),
        P("shard", None),
    )
    return jax.shard_map(
        on_device,
        mesh=mesh,
        in_specs=placed,
        out_specs=(P("shard", None), P("shard", None), P(), P("shard", None), P("shard", None)),
        check_vma=False,
    )
```

profile of v0, /device:TPU:0, one launch (start us, length us, event | category | flops | bytes accessed | tf_op | source)
XLA Modules:
  0.0 270.5 jit_solution(2345077583079396937)
XLA Ops:
  7.2 0.0 all-reduce.4.cloned.1.call-start
  7.2 16.8 %all_gather.10 = f32[2048,64]{0,1:T(8,128)S(1)} all-gather(f32[256,64]{0,1:T(8,128)} %param.13), channel_id=1, replica_groups=mesh['rep'=4,'shard'=8] {'shard'}, dimensions={0}, use_global_device_ids=true | all-gather | bytes 589824 | tf_op jit(solution)/shard_map/all_gather | solution.py:23
  24.0 12.6 %fusion.1 = f32[1024,64]{0,1:T(8,128)} fusion(f32[2048,64]{0,1:T(8,128)S(1)} %all_gather.10, f32[1024,2048]{1,0:T(8,128)} %param.11, f32[1,1024,2048]{2,1,0:T(8,128)} %param.10), kind=kOutput, calls=%fused_computation.4 | convolution fusion | flops 1612709888 | bytes 17563648 | tf_op jit(solution)/shard_map/dot_general | solution.py:26
  36.6 0.0 all-reduce.4.cloned.1.call-update
  36.6 0.0 reduce-scatter.2.cloned.1.call-start
  36.7 44.1 %all-reduce.4.cloned.1.call-done = f32[1024,64]{0,1:T(8,128)} async-done(((f32[1024,64]{0,1:T(8,128)}), f32[1024,64]{0,1:T(8,128)}) %all-reduce.4.cloned.1.call-update) | async-done | bytes 262160 | tf_op jit(solution)/shard_map/psum | solution.py:29
  80.8 1.4 fusion.7
  82.2 28.2 %psum.30 = f32[64,64]{0,1:T(8,128)S(1)} all-reduce(f32[64,64]{0,1:T(8,128)S(1)} %fusion.7), channel_id=1, replica_groups=mesh['rep'=4,'shard'=8] {'shard'}, use_global_device_ids=true, to_apply=%region_2.0 | all-reduce | flops 4096 | bytes 32768 | tf_op jit(solution)/shard_map/psum | solution.py:40
  110.3 0.1 copy.13
  110.4 5.8 %cholesky.16 = f32[64,64]{1,0:T(8,128)S(1)} custom-call(f32[64,64]{1,0:T(8,128)S(1)} %fusion.5), custom_call_target="Cholesky" | custom-call | tf_op jit(solution)/shard_map/jit(cholesky)/cholesky | solution.py:41
  116.3 0.6 compare_reduce_fusion
  116.9 0.7 fusion.2
  117.6 4.9 %custom-call.7 = f32[1,64,64]{1,2,0:T(8,128)S(1)} custom-call(f32[1,64,64]{2,1,0:T(8,128)S(1)} %fusion.2), custom_call_target="InvertDiagBlocksLowerTriangular" | custom-call | tf_op jit(solution)/shard_map/jit(_solve_triangular)/triangular_solve | solution.py:42
  122.5 1.4 fusion.3
  123.9 0.0 copy-start
  123.9 0.0 copy-start.1
  123.9 0.0 copy-start.2
  123.9 17.9 %fusion = f32[2048,64]{1,0:T(8,128)} fusion(f32[64,1024]{1,0:T(8,128)S(1)} %fusion.3, f32[1024,2048]{1,0:T(8,128)} %param.11, f32[1,1024,2048]{2,1,0:T(8,128)} %param.10), kind=kOutput, calls=%fused_computation.3 | convolution fusion | flops 1612709888 | bytes 17563648 | tf_op jit(solution)/shard_map/dot_general | solution.py:44
  141.9 0.0 reduce-scatter.2.cloned.1.call-update
  141.9 0.0 all-reduce.6.cloned.1.call-start
  141.9 0.0 copy-done
  141.9 0.0 copy-done.1
  142.0 0.9 bitcast_subtract_fusion.3
  142.8 28.8 %reduce-scatter.2.cloned.1.call-done = f32[256,64]{1,0:T(8,128)} async-done(((f32[2048,64]{1,0:T(8,128)}), f32[256,64]{1,0:T(8,128)}) %reduce-scatter.2.cloned.1.call-update) | async-done | bytes 65552 | tf_op jit(solution)/shard_map/reduce_scatter | solution.py:43
  171.6 0.0 all-reduce.6.cloned.1.call-update
  171.6 0.0 all-gather.2.cloned.1.call-start
  171.6 49.2 %all-reduce.6.cloned.1.call-done = (f32[128,1024]{1,0:T(8,128)}, f32[256,64]{1,0:T(8,128)}) async-done(((f32[128,1024]{1,0:T(8,128)}, f32[256,64]{1,0:T(8,128)}), (f32[128,1024]{1,0:T(8,128)}, f32[256,64]{1,0:T(8,128)})) %all-reduce.6.cloned.1.call-update) | async-done | bytes 589840 | tf_op jit(solution)/shard_map/psum | solution.py:29
  220.9 0.0 copy-done.2
  220.9 2.3 fusion.6
  223.1 0.0 all-gather.2.cloned.1.call-update
  223.1 22.0 %all_gather.11 = f32[2048,64]{1,0:T(8,128)S(1)} all-gather(f32[256,64]{1,0:T(8,128)} %get-tuple-element.6), channel_id=1, replica_groups=mesh['rep'=4,'shard'=8] {'shard'}, dimensions={0}, use_global_device_ids=true | all-gather | bytes 589824 | tf_op jit(solution)/shard_map/all_gather | solution.py:56
  245.2 15.7 %multiply_subtract_fusion = (f32[1024,2048]{1,0:T(8,128)}, f32[1024,2048]{1,0:T(8,128)}) fusion(f32[1024,2048]{1,0:T(8,128)} %param.11, f32[1024,2048]{1,0:T(8,128)} %param.12, f32[64,1024]{1,0:T(8,128)S(1)} %fusion.3, f32[2048,64]{1,0:T(8,128)S(1)} %all_gather.11), kind=kOutput, calls=%fused_computation.1 | convolution fusion | flops 1625292800 | bytes 34340864 | tf_op jit(solution)/shard_map/dot_general | solution.py:58
  260.9 0.0 all-gather.2.cloned.1.call-done
  260.9 3.1 %copy.19 = bf16[1024,1024]{1,0:T(8,128)(2,1)} copy(bf16[1024,1024]{1,0:T(8,128)(2,1)} %all-gather.2.cloned.1.call-done) | data formatting | bytes 4194304
  (2 shorter events, 0.0 us)
Async XLA Ops:
  7.2 73.6 %all-reduce.4.cloned.1.call-start = ((), (), s32[]{:S(2)}) async-start(), calls=%async_computation.2 | async-start | bytes 524288 | tf_op jit(solution)/shard_map/psum | solution.py:29
  36.6 134.9 %reduce-scatter.2.cloned.1.call-start = ((), (), s32[]{:S(2)}) async-start(), calls=%async_computation.3 | async-start | bytes 1179648 | tf_op jit(solution)/shard_map/reduce_scatter | solution.py:43
  123.9 18.1 %copy-start = (f32[128,1024]{1,0:T(8,128)S(1)}, f32[128,1024]{1,0:T(8,128)}, u32[]{:S(2)}) copy-start(f32[128,1024]{1,0:T(8,128)} %param.8) | copy-start | bytes 1572868
  123.9 18.1 %copy-start.1 = (f32[1,128,1024]{2,1,0:T(8,128)S(1)}, f32[1,128,1024]{2,1,0:T(8,128)}, u32[]{:S(2)}) copy-start(f32[1,128,1024]{2,1,0:T(8,128)} %param.7) | copy-start | bytes 1572868
  123.9 97.0 %copy-start.2 = (f32[128,1024]{1,0:T(8,128)S(1)}, f32[128,1024]{1,0:T(8,128)}, u32[]{:S(2)}) copy-start(f32[128,1024]{1,0:T(8,128)} %param.9) | copy-start | bytes 1572868
  141.9 79.0 %all-reduce.6.cloned.1.call-start = ((), (), s32[]{:S(2)}) async-start(), calls=%async_computation.4 | async-start | bytes 1310720 | tf_op jit(solution)/shard_map/psum | solution.py:29
  171.6 89.3 %all-gather.2.cloned.1.call-start = ((), (), s32[]{:S(2)}) async-start(), calls=%async_computation.1 | async-start | bytes 2359296 | tf_op jit(solution)/shard_map/all_gather | solution.py:15
Sparse Core Ops, SparseCore 0:
  36.7 43.9 all-reduce.3
  142.0 29.5 reduce-scatter.1
  175.5 45.3 all-reduce.5
  223.3 33.0 all-gather.1
where the time goes:
time: 271 us; the launch traced here: 270 us
  waiting for transfers between devices  122 us (45%)
  blocking collectives  67 us (25%)
  matrix products  49 us (18%)
  other arithmetic  15.2 us (6%)
  between operations  13.8 us (5%)
  local copies, waits for them, and re-layouts  3.17 us (1%)
    psum x2, waiting for transfers between devices, on_device(): dense_sum, factor = lax.psum((dense_diff, part_factor), 'rep')  93.3 us
    reduce_scatter x1, waiting for transfers between devices, on_device(): lax.psum_scatter(lax.dot_general(emb_diff, ortho_rows, (((0,), (0,)), (()...  28.8 us
    psum x1, blocking collectives, on_device(): gram_matrix = lax.psum(local_gram, 'shard')  28.2 us
    all_gather x1, blocking collectives, on_device(): coefficients = lax.all_gather(coeff_share, 'shard', axis=0, tiled=True)  22 us
    dot_general x1, matrix products, on_device(): lax.dot_general(emb_diff, ortho_rows, (((0,), (0,)), ((), ())), precision...  17.9 us
    all_gather x1, blocking collectives, on_device(): full_basis = lax.all_gather(proj_basis, 'shard', axis=0, tiled=True)  16.8 us
    dot_general x1, matrix products, on_device(): lax.dot_general(ortho_rows, coefficients, (((1,), (1,)), ((), ())), preci...  15.7 us
    dot_general x1, matrix products, on_device(): jnp.dot(emb_diff, full_basis, precision=highest, preferred_element_type=j...  12.6 us
  transfers between devices with their start and end apart: 4, of which 3 were waited for; matrix products, arithmetic and copies ran while one was open for 6% of the time, Pallas kernels for 0%

commit v1 on v0

v1 whole, which is shorter than its diff:
```python
import functools

import jax
import jax.numpy as jnp
from jax import lax
from jax.experimental import pallas as pl
from jax.experimental.pallas import tpu as pltpu
from jax.sharding import PartitionSpec as P

outer_rate = 0.7
momentum_rate = 0.9
highest = lax.Precision.HIGHEST
f32 = jnp.float32
bf16 = jnp.bfloat16
MESH = pl.DeviceIdType.MESH


def nesterov(grad, anchor, momentum):
    mom = momentum_rate * momentum + grad
    return anchor - outer_rate * (grad + momentum_rate * mom), mom


def plain(local_dense, anchor_dense, momentum_dense, local_emb, anchor_emb, momentum_emb, proj_basis):
    groups = lax.axis_size("rep")
    basis = lax.all_gather(proj_basis, "shard", axis=0, tiled=True)
    diff = anchor_emb - local_emb[0]
    part = jnp.dot(diff, basis, precision=highest, preferred_element_type=f32)
    dense_sum, factor = lax.psum((anchor_dense - local_dense[0], part), "rep")
    dense_new, dense_mom = nesterov(dense_sum / groups, anchor_dense, momentum_dense)
    weights = lax.all_gather(dense_new.astype(bf16), "shard", axis=0, tiled=True)
    across = functools.partial(
        lax.dot_general,
        dimension_numbers=(((0,), (0,)), ((), ())),
        precision=highest,
        preferred_element_type=f32,
    )
    gram = lax.psum(across(factor, factor), "shard")
    chol = jnp.linalg.cholesky(gram)
    ortho = jax.scipy.linalg.solve_triangular(chol, factor.T, lower=True).T
    share = lax.psum_scatter(across(diff, ortho), "shard", scatter_dimension=0, tiled=True)
    coeff = lax.all_gather(lax.psum(share, "rep"), "shard", axis=0, tiled=True)
    grad = (
        lax.dot_general(ortho, coeff, (((1,), (1,)), ((), ())), precision=highest, preferred_element_type=f32)
        / groups
    )
    emb_new, emb_mom = nesterov(grad, anchor_emb, momentum_emb)
    return (dense_new, dense_mom, weights, emb_new, emb_mom)


GROUPS = 4
CORES = 2
CHUNKS = GROUPS * CORES
N_COPIES = 48


def exchange_kernel(
    local_hbm, anchor_hbm, ld_ref, ad_ref, md_ref, basis_ref,
    h_ref, x_ref, dg_ref, dw_ref,
    lbuf, abuf, eh, el, bas, dd, drecv, f2, frecv, fsum, xt_ref, m_ref, mrecv1, mrecv2, msum, mrecv3, mz,
    gsend, grecv, gz, gram,
    lsem, asem, ssem, rsem,
):
    rep = lax.axis_index("rep")
    shard = lax.axis_index("shard")
    z, core = shard // CORES, shard % CORES
    other = 1 - core
    width = lbuf.shape[2]
    rank = basis_ref.shape[1]

    def rep_dev(j):
        return ((rep + j) % GROUPS, shard)

    def z_dev(j):
        return (rep, ((z + j) % GROUPS) * CORES + core)

    core_dev = (rep, z * CORES + other)
    started = []

    def send(src, dst, dev):
        i = len(started)
        copy = pltpu.make_async_remote_copy(
            src_ref=src, dst_ref=dst, send_sem=ssem.at[i], recv_sem=rsem.at[i],
            device_id=dev, device_id_type=MESH,
        )
        copy.start()
        started.append(copy)
        return copy

    def load(k, start):
        cols = pl.ds(pl.multiple_of(k * width, width), width)
        for src, dst, sem in ((local_hbm, lbuf, lsem), (anchor_hbm, abuf, asem)):
            copy = pltpu.make_async_copy(src.at[:, cols], dst.at[k], sem.at[k])
            if start:
                copy.start()
            else:
                copy.wait()

    @pl.loop(0, CHUNKS)
    def _(k):
        load(k, True)

    barrier = pltpu.get_barrier_semaphore()
    peers = [core_dev] + [rep_dev(j) for j in (1, 2, 3)] + [z_dev(j) for j in (1, 2, 3)]
    for dev in peers:
        pl.semaphore_signal(barrier, inc=1, device_id=dev, device_id_type=MESH)

    b = basis_ref[...]
    b_hi = b.astype(bf16)
    b_lo = (b - b_hi.astype(f32)).astype(bf16)
    bas[shard] = jnp.concatenate([b_hi, b_lo], axis=1)
    dd[...] = ad_ref[...] - ld_ref[...]
    pl.semaphore_wait(barrier, len(peers))

    basis_z = [send(bas.at[shard], bas.at[shard], z_dev(j)) for j in (1, 2, 3)]
    basis_core = [send(bas.at[shard], bas.at[shard], core_dev)]
    dense_rs = [send(dd.at[(rep + j) % GROUPS], drecv.at[j - 1], rep_dev(j)) for j in (1, 2, 3)]

    def split(k):
        load(k, False)
        e = abuf[k] - lbuf[k]
        hi = e.astype(bf16)
        eh[k] = hi
        el[k] = (e - hi.astype(f32)).astype(bf16)

    pl.loop(0, CHUNKS - 2)(split)
    for j in (1, 2, 3):
        basis_z[j - 1].wait_recv()
        at = ((z + GROUPS - j) % GROUPS) * CORES + core
        basis_core.append(send(bas.at[at], bas.at[at], core_dev))
    pl.loop(CHUNKS - 2, CHUNKS)(split)
    for copy in basis_core:
        copy.wait_recv()

    half = f2.shape[0] * f2.shape[1]
    lanes = f2.shape[2]
    piece = f2.shape[1]

    @pl.loop(0, GROUPS)
    def _(q):
        def summed(start):
            rows = pl.ds(pl.multiple_of(start + q * piece, piece), piece)
            total = jnp.zeros((piece, lanes), f32)
            for k in range(CHUNKS):
                total += jnp.dot(eh[k, rows, :], bas[k], preferred_element_type=f32)
                total += jnp.dot(el[k, rows, :], bas[k], preferred_element_type=f32)
            return total + pltpu.roll(total, rank, 1)

        lane = lax.broadcasted_iota(jnp.int32, (piece, lanes), 1)
        f2[q] = jnp.where(lane < rank, summed(0), summed(half))

    factor_rs = [send(f2.at[(rep + j) % GROUPS], frecv.at[j - 1], rep_dev(j)) for j in (1, 2, 3)]

    for copy in dense_rs:
        copy.wait_recv()
    dg_ref[rep] = (dd[rep] + drecv[0] + drecv[1] + drecv[2]) / GROUPS
    new_dense, _ = nesterov(dg_ref[rep], ad_ref[rep], md_ref[rep])
    dw_ref[core, rep, z] = new_dense.astype(bf16)

    for copy in factor_rs:
        copy.wait_recv()
    fsum[rep] = f2[rep] + frecv[0] + frecv[1] + frecv[2]
    factor_ag = [send(fsum.at[rep], fsum.at[rep], rep_dev(j)) for j in (1, 2, 3)]
    dense_ag = [send(dg_ref.at[rep], dg_ref.at[rep], rep_dev(j)) for j in (1, 2, 3)]
    mine = dw_ref.at[core, rep, z]
    weights_z = [send(mine, mine, z_dev(j)) for j in (1, 2, 3)]
    for copy in factor_ag:
        copy.wait_recv()

    lane = lax.broadcasted_iota(jnp.int32, (piece, lanes), 1)
    for q in range(GROUPS):
        here = fsum[q]
        there = pltpu.roll(here, rank, 1)
        for top, twice in ((0, jnp.where(lane < rank, here, there)), (half, jnp.where(lane < rank, there, here))):
            hi = twice.astype(bf16).astype(f32)
            x = jnp.where(lane < rank, hi, twice - hi)
            at = top + q * piece
            x_ref[at : at + piece, :] = x.astype(bf16)
            xt_ref[:, at : at + piece] = x.T.astype(bf16)

    g = jnp.dot(xt_ref[...], x_ref[...], preferred_element_type=f32)
    g = g[:rank] + g[rank:]
    g = g + pltpu.roll(g, rank, 1)
    fold = rank // 2
    lane_g = lax.broadcasted_iota(jnp.int32, (fold, lanes), 1)
    gsend[...] = jnp.where(lane_g < rank, g[:fold], g[fold:])
    gram_core = send(gsend, grecv, core_dev)

    @pl.loop(0, CHUNKS)
    def _(k):
        m = jnp.dot(xt_ref[...], eh[k], preferred_element_type=f32)
        m += jnp.dot(xt_ref[...], el[k], preferred_element_type=f32)
        m_ref[k] = m[:rank] + m[rank:]

    coeff_core = send(m_ref.at[pl.ds(other * GROUPS, GROUPS)], mrecv1, core_dev)
    gram_core.wait_recv()
    gz[z] = gsend[...] + grecv[...]
    gram_z = [send(gz.at[z], gz.at[z], z_dev(j)) for j in (1, 2, 3)]

    coeff_core.wait_recv()
    mrecv1[...] += m_ref[pl.ds(core * GROUPS, GROUPS)]
    coeff_rs = [send(mrecv1.at[(rep + j) % GROUPS], mrecv2.at[j - 1], rep_dev(j)) for j in (1, 2, 3)]

    for copy in weights_z:
        copy.wait_recv()
    ours = dw_ref.at[core, rep]
    weights_rep = [send(ours, ours, rep_dev(j)) for j in (1, 2, 3)]

    for copy in gram_z:
        copy.wait_recv()
    folded = gz[0] + gz[1] + gz[2] + gz[3]
    back = pltpu.roll(folded, rank, 1)
    gram[:fold] = folded
    gram[fold:] = back

    sub_i = lax.broadcasted_iota(jnp.int32, (rank, lanes), 0)
    lane_i = lax.broadcasted_iota(jnp.int32, (rank, lanes), 1)
    lane_1 = lax.broadcasted_iota(jnp.int32, (1, lanes), 1)

    @pl.loop(0, rank)
    def _(k):
        a = gram[...]
        row = gram[pl.ds(k, 1), :]
        at_k = lane_i == k
        col = jnp.sum(jnp.where(at_k, a, 0.0), axis=1, keepdims=True)
        pivot = jnp.sum(jnp.where(lane_1 == k, row, 0.0), axis=1, keepdims=True)
        scaled = jnp.where(lane_1 == k, 1.0, row) / pivot
        gram[...] = jnp.where(sub_i == k, scaled, jnp.where(at_k, 0.0, a) - col * scaled)

    for copy in coeff_rs:
        copy.wait_recv()
    msum[...] = (mrecv1[rep] + mrecv2[0] + mrecv2[1] + mrecv2[2]).reshape(msum.shape)
    coeff_z = [send(msum.at[(z + j) % GROUPS], mrecv3.at[j - 1], z_dev(j)) for j in (1, 2, 3)]
    for copy in coeff_z:
        copy.wait_recv()
    mz[z] = msum[z] + mrecv3[0] + mrecv3[1] + mrecv3[2]
    coeff_zag = [send(mz.at[z], mz.at[z], z_dev(j)) for j in (1, 2, 3)]
    for copy in coeff_zag:
        copy.wait_recv()
    h = jnp.dot(gram[:, :rank], mz[...].reshape(rank, width), precision=highest, preferred_element_type=f32)
    h = h / GROUPS
    h_hi = h.astype(bf16)
    own = core * GROUPS + rep
    h_ref[own, :rank, :] = h_hi
    h_ref[own, rank:, :] = (h - h_hi.astype(f32)).astype(bf16)
    h_rep = [send(h_ref.at[own], h_ref.at[own], rep_dev(j)) for j in (1, 2, 3)]
    h_core = [send(h_ref.at[own], h_ref.at[own], core_dev)]
    for j in (1, 2, 3):
        h_rep[j - 1].wait_recv()
        at = core * GROUPS + (rep + GROUPS - j) % GROUPS
        h_core.append(send(h_ref.at[at], h_ref.at[at], core_dev))

    for copy in weights_rep:
        copy.wait_recv()
    weights_core = send(dw_ref.at[core], dw_ref.at[core], core_dev)
    for copy in dense_ag + h_core + [weights_core]:
        copy.wait_recv()
    for copy in started:
        copy.wait_send()


def update_kernel(x_ref, h_ref, anchor_ref, mom_ref, dg_ref, ad_ref, md_ref, dw_ref,
                  dn_out, dm_out, dw_out, new_out, mom_out):
    x = x_ref[...]
    rank = h_ref.shape[1] // 2
    width = h_ref.shape[2]
    x2 = jnp.concatenate([x, x], axis=1)
    for k in range(h_ref.shape[0]):
        cols = slice(k * width, (k + 1) * width)
        hi, lo = h_ref[k, :rank, :], h_ref[k, rank:, :]
        grad = jnp.dot(x2, jnp.concatenate([hi, hi, lo, lo], axis=0), preferred_element_type=f32)
        new_out[:, cols], mom_out[:, cols] = nesterov(grad, anchor_ref[:, cols], mom_ref[:, cols])
    dn_out[...], dm_out[...] = nesterov(dg_ref[...], ad_ref[...], md_ref[...])
    dw_out[...] = dw_ref[...].reshape(dw_out.shape)


def fused(local_dense, anchor_dense, momentum_dense, local_emb, anchor_emb, momentum_emb, proj_basis):
    rows, cols = anchor_emb.shape
    drows, dcols = anchor_dense.shape
    rank = proj_basis.shape[1]
    width = cols // CHUNKS
    dq = drows // GROUPS
    piece = rows // 2 // GROUPS
    lanes = 2 * rank
    quarters = (GROUPS, dq, dcols)
    vmem = pl.BlockSpec(memory_space=pltpu.VMEM)
    hbm = pl.BlockSpec(memory_space=pltpu.HBM)
    S = jax.ShapeDtypeStruct
    h, x, dg, dw = pl.pallas_call(
        exchange_kernel,
        out_shape=(
            S((CHUNKS, lanes, width), bf16),
            S((rows, lanes), bf16),
            S(quarters, f32),
            S((CORES, GROUPS, GROUPS, dq, dcols), bf16),
        ),
        in_specs=[hbm, hbm] + [vmem] * 4,
        out_specs=(vmem,) * 4,
        scratch_shapes=[
            pltpu.VMEM((CHUNKS, rows, width), f32),
            pltpu.VMEM((CHUNKS, rows, width), f32),
            pltpu.VMEM((CHUNKS, rows, width), bf16),
            pltpu.VMEM((CHUNKS, rows, width), bf16),
            pltpu.VMEM((CHUNKS, width, lanes), bf16),
            pltpu.VMEM(quarters, f32),
            pltpu.VMEM((3, dq, dcols), f32),
            pltpu.VMEM((GROUPS, piece, lanes), f32),
            pltpu.VMEM((3, piece, lanes), f32),
            pltpu.VMEM((GROUPS, piece, lanes), f32),
            pltpu.VMEM((lanes, rows), bf16),
            pltpu.VMEM((CHUNKS, rank, width), f32),
            pltpu.VMEM((GROUPS, rank, width), f32),
            pltpu.VMEM((3, rank, width), f32),
            pltpu.VMEM((GROUPS, rank // GROUPS, width), f32),
            pltpu.VMEM((3, rank // GROUPS, width), f32),
            pltpu.VMEM((GROUPS, rank // GROUPS, width), f32),
            pltpu.VMEM((rank // 2, lanes), f32),
            pltpu.VMEM((rank // 2, lanes), f32),
            pltpu.VMEM((GROUPS, rank // 2, lanes), f32),
            pltpu.VMEM((rank, lanes), f32),
            pltpu.SemaphoreType.DMA((CHUNKS,)),
            pltpu.SemaphoreType.DMA((CHUNKS,)),
            pltpu.SemaphoreType.DMA((N_COPIES,)),
            pltpu.SemaphoreType.DMA((N_COPIES,)),
        ],
        compiler_params=pltpu.CompilerParams(
            collective_id=0, has_side_effects=True, vmem_limit_bytes=52 * 1024 * 1024
        ),
    )(
        local_emb[0], anchor_emb, local_dense[0].reshape(quarters), anchor_dense.reshape(quarters),
        momentum_dense.reshape(quarters), proj_basis,
    )

    steps = CHUNKS
    block = (rows // steps, cols)
    dense_block = (drows // steps, dcols)
    by_row = lambda shape: pl.BlockSpec(shape, lambda i: (i, 0))
    return pl.pallas_call(
        update_kernel,
        grid=(steps,),
        out_shape=(
            S(anchor_dense.shape, f32),
            S(anchor_dense.shape, f32),
            S((drows * CHUNKS, dcols), bf16),
            S(anchor_emb.shape, f32),
            S(anchor_emb.shape, f32),
        ),
        in_specs=[
            by_row((rows // steps, lanes)),
            pl.BlockSpec((CHUNKS, lanes, width), lambda i: (0, 0, 0)),
            by_row(block),
            by_row(block),
            by_row(dense_block),
            by_row(dense_block),
            by_row(dense_block),
            pl.BlockSpec((1, GROUPS, 1, dq, dcols), lambda i: (i % CORES, 0, i // CORES, 0, 0)),
        ],
        out_specs=(
            by_row(dense_block),
            by_row(dense_block),
            by_row((drows, dcols)),
            by_row(block),
            by_row(block),
        ),
        compiler_params=pltpu.CompilerParams(vmem_limit_bytes=40 * 1024 * 1024),
    )(x, h, anchor_emb, momentum_emb, dg.reshape(anchor_dense.shape), anchor_dense, momentum_dense, dw)


def solution(mesh):
    fits = mesh.shape["rep"] == GROUPS and mesh.shape["shard"] == CHUNKS
    placed = (
        P("rep", "shard", None),
        P("shard", None),
        P("shard", None),
        P("rep", "shard", None),
        P("shard", None),
        P("shard", None),
        P("shard", None),
    )
    return jax.shard_map(
        fused if fits else plain,
        mesh=mesh,
        in_specs=placed,
        out_specs=(P("shard", None), P("shard", None), P(), P("shard", None), P("shard", None)),
        check_vma=False,
    )
```

time: 271 us -> 75.5 us (0.28)
  waiting for transfers between devices: 122 us -> 0 us
  Pallas kernels: 0 us -> 70.7 us
  blocking collectives: 67 us -> 0 us
  matrix products: 49 us -> 0 us
  other arithmetic: 15.2 us -> 0 us
  between operations: 13.8 us -> 0.69 us
    psum x2 -> x0, waiting for transfers between devices: 93.3 us -> none  [on_device(): dense_sum, factor = lax.psum((dense_diff, part_factor), 'rep')]
    pallas_call x0 -> x2, Pallas kernels: none -> 70.7 us  [the longest x1 58.7 us: fused(): pl.pallas_call(exchange_kernel, out_shape=(S((CHUNKS, lanes, width), bf16...]
    dot_general x4 -> x0, matrix products: 47.6 us -> none  [the longest x1 17.9 us: on_device(): lax.dot_general(emb_diff, ortho_rows, (((0,), (0,)), ((), ())), precision...]
    all_gather x2 -> x0, blocking collectives: 38.8 us -> none  [the longest x1 22 us: on_device(): coefficients = lax.all_gather(coeff_share, 'shard', axis=0, tiled=True)]
    reduce_scatter x1 -> x0, waiting for transfers between devices: 28.8 us -> none  [on_device(): lax.psum_scatter(lax.dot_general(emb_diff, ortho_rows, (((0,), (0,)), (()...]
    psum x1 -> x0, blocking collectives: 28.2 us -> none  [on_device(): gram_matrix = lax.psum(local_gram, 'shard')]
    another operation x5 -> x0, other arithmetic: 12.1 us -> none  [the longest x3 6.52 us: on_device(): chol_lower = jnp.linalg.cholesky(gram_matrix)]
  transfers between devices with their start and end apart: 4 -> 0, of which waited for: 3 -> 0; matrix products, arithmetic and copies ran while one was open for 6% -> 0% of each run, Pallas kernels for 0% -> 0%
where the time goes in v1:
time: 75.5 us; the launch traced here: 75 us
  Pallas kernels  70.7 us (94%)
  local copies, waits for them, and re-layouts  3.57 us (5%)
    pallas_call x1, Pallas kernels, fused(): pl.pallas_call(exchange_kernel, out_shape=(S((CHUNKS, lanes, width), bf16...  58.7 us
    pallas_call x1, Pallas kernels, fused(): pl.pallas_call(update_kernel, grid=(steps,), out_shape=(S(anchor_dense.sh...  12.1 us
    unnamed x11, local copies, waits for them, and re-layouts  3.57 us

profile of v1, /device:TPU:0, one launch (start us, length us, event | category | flops | bytes accessed | tf_op | source)
XLA Modules:
  0.0 75.0 jit_solution(13369756959040478514)
XLA Ops:
  0.6 0.9 %copy.12.basis_ref = f32[256,64]{1,0:T(8,128)S(1)} copy(f32[256,64]{0,1:T(8,128)} %param.13) | data formatting | bytes 131072 | tf_op args[6]
  1.6 0.0 copy-start.4
  1.6 1.0 %copy-done.4 = f32[1,128,1024]{2,1,0:T(8,128)S(1)} copy-done((f32[1,128,1024]{2,1,0:T(8,128)S(1)}, f32[1,128,1024]{2,1,0:T(8,128)}, u32[]{:S(2)}) %copy-start.4) | copy-done | bytes 524312
  2.6 0.0 copy-start
  2.6 0.0 copy-start.2
  2.6 0.0 copy-start.3
  2.6 58.7 %shard_map.110 = (bf16[8,128,256]{2,1,0:T(8,128)(2,1)S(1)}, bf16[1024,128]{1,0:T(8,128)(2,1)S(1)}, f32[4,32,1024]{2,1,0:T(8,128)S(1)}, bf16[2,4,4,32,1024]{4,3,2,1,0:T(8,128)(2,1)}) custom-call(f32[1024,2048]{1,0:T(8,128)} %bitcast.9, f32[1024,2048]{1,0:T(8,128)} %anchor_ref.1, f32[4,32,1024]{2,1,0:T(8,128)S(1)} %bitcast.7, f32[4,32,1024]{2,1,0:T(8,128)} %bitcast.5, ...), custom_call_target="tpu_custom_call" | custom-call | tf_op jit(solution)/shard_map/pallas_call | solution.py:288
  61.3 0.0 copy-done
  61.3 0.0 copy-done.2
  61.3 0.0 copy-done.3
  61.3 0.0 copy-start.1
  61.3 1.6 %copy-done.1 = bf16[2,4,4,32,1024]{4,3,2,1,0:T(8,128)(2,1)S(1)} copy-done((bf16[2,4,4,32,1024]{4,3,2,1,0:T(8,128)(2,1)S(1)}, bf16[2,4,4,32,1024]{4,3,2,1,0:T(8,128)(2,1)}, u32[]{:S(2)}) %copy-start.1) | copy-done | bytes 2097176
  62.9 12.1 %shard_map.111 = (f32[128,1024]{1,0:T(8,128)}, f32[128,1024]{1,0:T(8,128)}, bf16[1024,1024]{1,0:T(8,128)(2,1)}, f32[1024,2048]{1,0:T(8,128)}, f32[1024,2048]{1,0:T(8,128)}) custom-call(bf16[1024,128]{1,0:T(8,128)(2,1)S(1)} %get-tuple-element.9.x_ref, bf16[8,128,256]{2,1,0:T(8,128)(2,1)S(1)} %get-tuple-element.10.h_ref, f32[1024,2048]{1,0:T(8,128)S(1)} %copy-done, ...), custom_call_target="tpu_custom_call" | custom-call | tf_op jit(solution)/shard_map/pallas_call | solution.py:337
Async XLA Ops:
  1.6 1.0 %copy-start.4 = (f32[1,128,1024]{2,1,0:T(8,128)S(1)}, f32[1,128,1024]{2,1,0:T(8,128)}, u32[]{:S(2)}) copy-start(f32[1,128,1024]{2,1,0:T(8,128)} %param.7) | copy-start | bytes 1572868
  2.6 58.7 %copy-start = (f32[1024,2048]{1,0:T(8,128)S(1)}, f32[1024,2048]{1,0:T(8,128)}, u32[]{:S(2)}) copy-start(f32[1024,2048]{1,0:T(8,128)} %anchor_ref.1) | copy-start | bytes 25165828
  2.6 58.7 %copy-start.2 = (f32[128,1024]{1,0:T(8,128)S(1)}, f32[128,1024]{1,0:T(8,128)}, u32[]{:S(2)}) copy-start(f32[128,1024]{1,0:T(8,128)} %ad_ref.1) | copy-start | bytes 1572868
  2.6 58.7 %copy-start.3 = (f32[128,1024]{1,0:T(8,128)S(1)}, f32[128,1024]{1,0:T(8,128)}, u32[]{:S(2)}) copy-start(f32[128,1024]{1,0:T(8,128)} %md_ref.1) | copy-start | bytes 1572868
  61.3 1.6 %copy-start.1 = (bf16[2,4,4,32,1024]{4,3,2,1,0:T(8,128)(2,1)S(1)}, bf16[2,4,4,32,1024]{4,3,2,1,0:T(8,128)(2,1)}, u32[]{:S(2)}) copy-start(bf16[2,4,4,32,1024]{4,3,2,1,0:T(8,128)(2,1)} %get-tuple-element.12.dw_ref) | copy-start | bytes 6291460

commit v2 on v1

--- a/solution.py
+++ b/solution.py
@@ -50,15 +50,17 @@
 GROUPS = 4
 CORES = 2
 CHUNKS = GROUPS * CORES
-N_COPIES = 48
+N_COPIES = 64
+LIMIT1 = 28 * 1024 * 1024
+LIMIT2 = 28 * 1024 * 1024
 
 
 def exchange_kernel(
-    local_hbm, anchor_hbm, ld_ref, ad_ref, md_ref, basis_ref,
-    h_ref, x_ref, dg_ref, dw_ref,
-    lbuf, abuf, eh, el, bas, dd, drecv, f2, frecv, fsum, xt_ref, m_ref, mrecv1, mrecv2, msum, mrecv3, mz,
+    local_hbm, anchor_hbm, momentum_hbm, ld_ref, ad_ref, md_ref, basis_ref,
+    h_ref, x_ref, dg_ref, dw_ref, abuf, mbuf,
+    lbuf, eh, el, bas, dd, drecv, f2, frecv, fsum, xt_ref, m_ref, mrecv1, mrecv2, msum, mrecv3, mz,
     gsend, grecv, gz, gram,
-    lsem, asem, ssem, rsem,
+    lsem, asem, msem, ssem, rsem,
 ):
     rep = lax.axis_index("rep")
     shard = lax.axis_index("shard")
@@ -86,9 +88,12 @@
         started.append(copy)
         return copy
 
-    def load(k, start):
+    differences = ((local_hbm, lbuf, lsem), (anchor_hbm, abuf, asem))
+    momenta = ((momentum_hbm, mbuf, msem),)
+
+    def load(k, start, arrays=differences):
         cols = pl.ds(pl.multiple_of(k * width, width), width)
-        for src, dst, sem in ((local_hbm, lbuf, lsem), (anchor_hbm, abuf, asem)):
+        for src, dst, sem in arrays:
             copy = pltpu.make_async_copy(src.at[:, cols], dst.at[k], sem.at[k])
             if start:
                 copy.start()
@@ -128,6 +133,11 @@
         at = ((z + GROUPS - j) % GROUPS) * CORES + core
         basis_core.append(send(bas.at[at], bas.at[at], core_dev))
     pl.loop(CHUNKS - 2, CHUNKS)(split)
+
+    @pl.loop(0, CHUNKS)
+    def _(k):
+        load(k, True, momenta)
+
     for copy in basis_core:
         copy.wait_recv()
 
@@ -135,18 +145,15 @@
     lanes = f2.shape[2]
     piece = f2.shape[1]
 
-    @pl.loop(0, GROUPS)
-    def _(q):
-        def summed(start):
-            rows = pl.ds(pl.multiple_of(start + q * piece, piece), piece)
-            total = jnp.zeros((piece, lanes), f32)
-            for k in range(CHUNKS):
-                total += jnp.dot(eh[k, rows, :], bas[k], preferred_element_type=f32)
-                total += jnp.dot(el[k, rows, :], bas[k], preferred_element_type=f32)
-            return total + pltpu.roll(total, rank, 1)
-
-        lane = lax.broadcasted_iota(jnp.int32, (piece, lanes), 1)
-        f2[q] = jnp.where(lane < rank, summed(0), summed(half))
+    def summed(start):
+        total = jnp.zeros((half, lanes), f32)
+        for k in range(CHUNKS):
+            total += jnp.dot(eh[k, start : start + half, :], bas[k], preferred_element_type=f32)
+            total += jnp.dot(el[k, start : start + half, :], bas[k], preferred_element_type=f32)
+        return total + pltpu.roll(total, rank, 1)
+
+    lane_f = lax.broadcasted_iota(jnp.int32, (half, lanes), 1)
+    f2[...] = jnp.where(lane_f < rank, summed(0), summed(half)).reshape(f2.shape)
 
     factor_rs = [send(f2.at[(rep + j) % GROUPS], frecv.at[j - 1], rep_dev(j)) for j in (1, 2, 3)]
 
@@ -185,6 +192,12 @@
     gsend[...] = jnp.where(lane_g < rank, g[:fold], g[fold:])
     gram_core = send(gsend, grecv, core_dev)
 
+    for copy in weights_z:
+        copy.wait_recv()
+    first, second = pl.ds(0, GROUPS // 2), pl.ds(GROUPS // 2, GROUPS // 2)
+    ours = dw_ref.at[core, rep, first]
+    weights_first = [send(ours, ours, rep_dev(j)) for j in (1, 2, 3)]
+
     @pl.loop(0, CHUNKS)
     def _(k):
         m = jnp.dot(xt_ref[...], eh[k], preferred_element_type=f32)
@@ -200,10 +213,8 @@
     mrecv1[...] += m_ref[pl.ds(core * GROUPS, GROUPS)]
     coeff_rs = [send(mrecv1.at[(rep + j) % GROUPS], mrecv2.at[j - 1], rep_dev(j)) for j in (1, 2, 3)]
 
-    for copy in weights_z:
-        copy.wait_recv()
-    ours = dw_ref.at[core, rep]
-    weights_rep = [send(ours, ours, rep_dev(j)) for j in (1, 2, 3)]
+    ours = dw_ref.at[core, rep, second]
+    weights_second = [send(ours, ours, rep_dev(j)) for j in (1, 2, 3)]
 
     for copy in gram_z:
         copy.wait_recv()
@@ -216,24 +227,37 @@
     lane_i = lax.broadcasted_iota(jnp.int32, (rank, lanes), 1)
     lane_1 = lax.broadcasted_iota(jnp.int32, (1, lanes), 1)
 
-    @pl.loop(0, rank)
-    def _(k):
+    def pick(values, at):
+        return jnp.sum(jnp.where(at, values, 0.0), axis=1, keepdims=True)
+
+    def eliminate_two(pair):
+        k = pair * 2
         a = gram[...]
-        row = gram[pl.ds(k, 1), :]
-        at_k = lane_i == k
-        col = jnp.sum(jnp.where(at_k, a, 0.0), axis=1, keepdims=True)
-        pivot = jnp.sum(jnp.where(lane_1 == k, row, 0.0), axis=1, keepdims=True)
-        scaled = jnp.where(lane_1 == k, 1.0, row) / pivot
-        gram[...] = jnp.where(sub_i == k, scaled, jnp.where(at_k, 0.0, a) - col * scaled)
-
+        row0, row1 = gram[pl.ds(k, 1), :], gram[pl.ds(k + 1, 1), :]
+        at0, at1 = lane_i == k, lane_i == k + 1
+        one0, one1 = lane_1 == k, lane_1 == k + 1
+        col0, col1 = pick(a, at0), pick(a, at1)
+        s00, s01, s10, s11 = pick(row0, one0), pick(row0, one1), pick(row1, one0), pick(row1, one1)
+        p0 = jnp.where(one0, 1.0, row0) / s00
+        q01 = s01 / s00
+        row1 = jnp.where(one0, 0.0, row1) - s10 * p0
+        p1 = jnp.where(one1, 1.0, row1) / (s11 - s10 * q01)
+        p0 = jnp.where(one1, 0.0, p0)
+        col1 = col1 - col0 * q01
+        rest = jnp.where(at0 | at1, 0.0, a) - col0 * p0 - col1 * p1
+        gram[...] = jnp.where(sub_i == k, p0 - q01 * p1, jnp.where(sub_i == k + 1, p1, rest))
+
+    pl.loop(0, rank // 4)(eliminate_two)
     for copy in coeff_rs:
         copy.wait_recv()
     msum[...] = (mrecv1[rep] + mrecv2[0] + mrecv2[1] + mrecv2[2]).reshape(msum.shape)
     coeff_z = [send(msum.at[(z + j) % GROUPS], mrecv3.at[j - 1], z_dev(j)) for j in (1, 2, 3)]
+    pl.loop(rank // 4, 3 * rank // 8)(eliminate_two)
     for copy in coeff_z:
         copy.wait_recv()
     mz[z] = msum[z] + mrecv3[0] + mrecv3[1] + mrecv3[2]
     coeff_zag = [send(mz.at[z], mz.at[z], z_dev(j)) for j in (1, 2, 3)]
+    pl.loop(3 * rank // 8, rank // 2)(eliminate_two)
     for copy in coeff_zag:
         copy.wait_recv()
     h = jnp.dot(gram[:, :rank], mz[...].reshape(rank, width), precision=highest, preferred_element_type=f32)
@@ -249,28 +273,66 @@
         at = core * GROUPS + (rep + GROUPS - j) % GROUPS
         h_core.append(send(h_ref.at[at], h_ref.at[at], core_dev))
 
-    for copy in weights_rep:
-        copy.wait_recv()
-    weights_core = send(dw_ref.at[core], dw_ref.at[core], core_dev)
-    for copy in dense_ag + h_core + [weights_core]:
-        copy.wait_recv()
+    weights_core = []
+    for part, arrivals in ((first, weights_first), (second, weights_second)):
+        for copy in arrivals:
+            copy.wait_recv()
+        here = dw_ref.at[core, :, part]
+        weights_core.append(send(here, here, core_dev))
+    for copy in dense_ag + h_core + weights_core:
+        copy.wait_recv()
+
+    @pl.loop(0, CHUNKS)
+    def _(k):
+        load(k, False, momenta)
+
     for copy in started:
         copy.wait_send()
 
 
 def update_kernel(x_ref, h_ref, anchor_ref, mom_ref, dg_ref, ad_ref, md_ref, dw_ref,
-                  dn_out, dm_out, dw_out, new_out, mom_out):
-    x = x_ref[...]
+                  dn_out, dm_out, dw_out, new_out, mom_out, nbuf, pbuf, nsem, psem, wsem):
     rank = h_ref.shape[1] // 2
     width = h_ref.shape[2]
-    x2 = jnp.concatenate([x, x], axis=1)
-    for k in range(h_ref.shape[0]):
-        cols = slice(k * width, (k + 1) * width)
+    rows = x_ref.shape[0]
+    step = rows // 4
+
+    def weights(at):
+        return pltpu.make_async_copy(
+            dw_ref.at[at % CORES, :, at // CORES], dw_out.at[at // CORES, at % CORES], wsem.at[at]
+        )
+
+    def out(k):
+        cols = pl.ds(k * width, width)
+        return (
+            pltpu.make_async_copy(nbuf.at[k % 2], new_out.at[:, cols], nsem.at[k % 2]),
+            pltpu.make_async_copy(pbuf.at[k % 2], mom_out.at[:, cols], psem.at[k % 2]),
+        )
+
+    for at in range(CHUNKS):
+        weights(at).start()
+    for k in range(CHUNKS):
         hi, lo = h_ref[k, :rank, :], h_ref[k, rank:, :]
-        grad = jnp.dot(x2, jnp.concatenate([hi, hi, lo, lo], axis=0), preferred_element_type=f32)
-        new_out[:, cols], mom_out[:, cols] = nesterov(grad, anchor_ref[:, cols], mom_ref[:, cols])
+        right = jnp.concatenate([hi, hi, lo, lo], axis=0)
+        if k >= 2:
+            for copy in out(k - 2):
+                copy.wait()
+
+        @pl.loop(0, rows // step)
+        def _(t):
+            at = pl.ds(pl.multiple_of(t * step, step), step)
+            x = x_ref[at, :]
+            grad = jnp.dot(jnp.concatenate([x, x], axis=1), right, preferred_element_type=f32)
+            nbuf[k % 2, at, :], pbuf[k % 2, at, :] = nesterov(grad, anchor_ref[k, at, :], mom_ref[k, at, :])
+
+        for copy in out(k):
+            copy.start()
     dn_out[...], dm_out[...] = nesterov(dg_ref[...], ad_ref[...], md_ref[...])
-    dw_out[...] = dw_ref[...].reshape(dw_out.shape)
+    for k in (CHUNKS - 2, CHUNKS - 1):
+        for copy in out(k):
+            copy.wait()
+    for at in range(CHUNKS):
+        weights(at).wait()
 
 
 def fused(local_dense, anchor_dense, momentum_dense, local_emb, anchor_emb, momentum_emb, proj_basis):
@@ -285,18 +347,19 @@
     vmem = pl.BlockSpec(memory_space=pltpu.VMEM)
     hbm = pl.BlockSpec(memory_space=pltpu.HBM)
     S = jax.ShapeDtypeStruct
-    h, x, dg, dw = pl.pallas_call(
+    h, x, dg, dw, anchor, momentum = pl.pallas_call(
         exchange_kernel,
         out_shape=(
             S((CHUNKS, lanes, width), bf16),
             S((rows, lanes), bf16),
             S(quarters, f32),
             S((CORES, GROUPS, GROUPS, dq, dcols), bf16),
+            S((CHUNKS, rows, width), f32),
+            S((CHUNKS, rows, width), f32),
         ),
-        in_specs=[hbm, hbm] + [vmem] * 4,
-        out_specs=(vmem,) * 4,
+        in_specs=[hbm] * 3 + [vmem] * 4,
+        out_specs=(vmem,) * 6,
         scratch_shapes=[
-            pltpu.VMEM((CHUNKS, rows, width), f32),
             pltpu.VMEM((CHUNKS, rows, width), f32),
             pltpu.VMEM((CHUNKS, rows, width), bf16),
             pltpu.VMEM((CHUNKS, rows, width), bf16),
@@ -319,50 +382,39 @@
             pltpu.VMEM((rank, lanes), f32),
             pltpu.SemaphoreType.DMA((CHUNKS,)),
             pltpu.SemaphoreType.DMA((CHUNKS,)),
+            pltpu.SemaphoreType.DMA((CHUNKS,)),
             pltpu.SemaphoreType.DMA((N_COPIES,)),
             pltpu.SemaphoreType.DMA((N_COPIES,)),
         ],
         compiler_params=pltpu.CompilerParams(
-            collective_id=0, has_side_effects=True, vmem_limit_bytes=52 * 1024 * 1024
+            collective_id=0, has_side_effects=True, vmem_limit_bytes=LIMIT1
         ),
     )(
-        local_emb[0], anchor_emb, local_dense[0].reshape(quarters), anchor_dense.reshape(quarters),
+        local_emb[0], anchor_emb, momentum_emb, local_dense[0].reshape(quarters), anchor_dense.reshape(quarters),
         momentum_dense.reshape(quarters), proj_basis,
     )
 
-    steps = CHUNKS
-    block = (rows // steps, cols)
-    dense_block = (drows // steps, dcols)
-    by_row = lambda shape: pl.BlockSpec(shape, lambda i: (i, 0))
-    return pl.pallas_call(
+    dn, dm, weights, new, mom = pl.pallas_call(
         update_kernel,
-        grid=(steps,),
         out_shape=(
             S(anchor_dense.shape, f32),
             S(anchor_dense.shape, f32),
-            S((drows * CHUNKS, dcols), bf16),
+            S((GROUPS, CORES, GROUPS, dq, dcols), bf16),
             S(anchor_emb.shape, f32),
             S(anchor_emb.shape, f32),
         ),
-        in_specs=[
-            by_row((rows // steps, lanes)),
-            pl.BlockSpec((CHUNKS, lanes, width), lambda i: (0, 0, 0)),
-            by_row(block),
-            by_row(block),
-            by_row(dense_block),
-            by_row(dense_block),
-            by_row(dense_block),
-            pl.BlockSpec((1, GROUPS, 1, dq, dcols), lambda i: (i % CORES, 0, i // CORES, 0, 0)),
+        in_specs=[vmem] * 8,
+        out_specs=(vmem, vmem, hbm, hbm, hbm),
+        scratch_shapes=[
+            pltpu.VMEM((2, rows, width), f32),
+            pltpu.VMEM((2, rows, width), f32),
+            pltpu.SemaphoreType.DMA((2,)),
+            pltpu.SemaphoreType.DMA((2,)),
+            pltpu.SemaphoreType.DMA((CHUNKS,)),
         ],
-        out_specs=(
-            by_row(dense_block),
-            by_row(dense_block),
-            by_row((drows, dcols)),
-            by_row(block),
-            by_row(block),
-        ),
-        compiler_params=pltpu.CompilerParams(vmem_limit_bytes=40 * 1024 * 1024),
-    )(x, h, anchor_emb, momentum_emb, dg.reshape(anchor_dense.shape), anchor_dense, momentum_dense, dw)
+        compiler_params=pltpu.CompilerParams(vmem_limit_bytes=LIMIT2),
+    )(x, h, anchor, momentum, dg.reshape(anchor_dense.shape), anchor_dense, momentum_dense, dw)
+    return dn, dm, weights.reshape(drows * CHUNKS, dcols), new, mom
 
 
 def solution(mesh):

time: 75.5 us -> 71.2 us (0.943)
  Pallas kernels: 70.7 us -> 66.2 us
    pallas_call x1, Pallas kernels: 58.7 us -> 55.6 us  [fused(): pl.pallas_call(exchange_kernel, out_shape=(S((CHUNKS, lanes, width), bf16...]
    pallas_call x1, Pallas kernels: 12.1 us -> 10.6 us  [fused(): pl.pallas_call(update_kernel, out_shape=(S(anchor_dense.shape, f32), S(an...]
where the time goes in v2:
time: 71.2 us; the launch traced here: 70.9 us
  Pallas kernels  66.2 us (93%)
  local copies, waits for them, and re-layouts  4.06 us (6%)
    pallas_call x1, Pallas kernels, fused(): pl.pallas_call(exchange_kernel, out_shape=(S((CHUNKS, lanes, width), bf16...  55.6 us
    pallas_call x1, Pallas kernels, fused(): pl.pallas_call(update_kernel, out_shape=(S(anchor_dense.shape, f32), S(an...  10.6 us
    unnamed x11, local copies, waits for them, and re-layouts  4.06 us

profile of v2, /device:TPU:0, one launch (start us, length us, event | category | flops | bytes accessed | tf_op | source)
XLA Modules:
  0.0 70.9 jit_solution(17657810087035503579)
XLA Ops:
  0.6 0.9 %copy.12.basis_ref = f32[256,64]{1,0:T(8,128)S(1)} copy(f32[256,64]{0,1:T(8,128)} %param.13) | data formatting | bytes 131072 | tf_op args[6]
  1.6 0.0 copy-start
  1.6 1.0 %copy-done = f32[128,1024]{1,0:T(8,128)S(1)} copy-done((f32[128,1024]{1,0:T(8,128)S(1)}, f32[128,1024]{1,0:T(8,128)}, u32[]{:S(2)}) %copy-start) | copy-done | bytes 524312
  2.6 0.0 copy-start.2
  2.6 1.0 %copy-done.2 = f32[128,1024]{1,0:T(8,128)S(1)} copy-done((f32[128,1024]{1,0:T(8,128)S(1)}, f32[128,1024]{1,0:T(8,128)}, u32[]{:S(2)}) %copy-start.2) | copy-done | bytes 524312
  3.7 0.0 copy-start.4
  3.7 1.0 %copy-done.4 = f32[1,128,1024]{2,1,0:T(8,128)S(1)} copy-done((f32[1,128,1024]{2,1,0:T(8,128)S(1)}, f32[1,128,1024]{2,1,0:T(8,128)}, u32[]{:S(2)}) %copy-start.4) | copy-done | bytes 524312
  4.7 0.0 copy-start.1
  4.7 0.0 copy-start.3
  4.7 55.6 %shard_map.110 = (bf16[8,128,256]{2,1,0:T(8,128)(2,1)S(1)}, bf16[1024,128]{1,0:T(8,128)(2,1)S(1)}, f32[4,32,1024]{2,1,0:T(8,128)S(1)}, bf16[2,4,4,32,1024]{4,3,2...) custom-call(f32[1024,2048]{1,0:T(8,128)} %bitcast.10, f32[1024,2048]{1,0:T(8,128)} %anchor_hbm.1, ...), custom_call_target="tpu_custom_call" | custom-call | tf_op jit(solution)/shard_map/pallas_call | solution.py:350
  60.3 0.0 copy-done.1
  60.3 0.0 copy-done.3
  60.3 10.6 %shard_map.111 = (f32[128,1024]{1,0:T(8,128)}, f32[128,1024]{1,0:T(8,128)}, bf16[4,2,4,32,1024]{4,3,2,1,0:T(8,128)(2,1)}, f32[1024,2048]{1,0:T(8,128)}, f32[1024,2048]{1,0:T(8,128)}) custom-call(bf16[1024,128]{1,0:T(8,128)(2,1)S(1)} %get-tuple-element.16.x_ref, bf16[8,128,256]{2,1,0:T(8,128)(2,1)S(1)} %get-tuple-element.17.h_ref, ...), custom_call_target="tpu_custom_call" | custom-call | tf_op jit(solution)/shard_map/pallas_call | solution.py:397
Async XLA Ops:
  1.6 1.0 %copy-start = (f32[128,1024]{1,0:T(8,128)S(1)}, f32[128,1024]{1,0:T(8,128)}, u32[]{:S(2)}) copy-start(f32[128,1024]{1,0:T(8,128)} %ad_ref.1) | copy-start | bytes 1572868
  2.6 1.0 %copy-start.2 = (f32[128,1024]{1,0:T(8,128)S(1)}, f32[128,1024]{1,0:T(8,128)}, u32[]{:S(2)}) copy-start(f32[128,1024]{1,0:T(8,128)} %md_ref.1) | copy-start | bytes 1572868
  3.7 1.0 %copy-start.4 = (f32[1,128,1024]{2,1,0:T(8,128)S(1)}, f32[1,128,1024]{2,1,0:T(8,128)}, u32[]{:S(2)}) copy-start(f32[1,128,1024]{2,1,0:T(8,128)} %param.7) | copy-start | bytes 1572868
  4.7 55.6 %copy-start.1 = (f32[128,1024]{1,0:T(8,128)S(1)}, f32[128,1024]{1,0:T(8,128)}, u32[]{:S(2)}) copy-start(f32[128,1024]{1,0:T(8,128)} %ad_ref.1) | copy-start | bytes 1572868
  4.7 55.6 %copy-start.3 = (f32[128,1024]{1,0:T(8,128)S(1)}, f32[128,1024]{1,0:T(8,128)}, u32[]{:S(2)}) copy-start(f32[128,1024]{1,0:T(8,128)} %md_ref.1) | copy-start | bytes 1572868

commit v3 on v2

--- a/solution.py
+++ b/solution.py
@@ -56,18 +56,18 @@
 
 
 def exchange_kernel(
-    local_hbm, anchor_hbm, momentum_hbm, ld_ref, ad_ref, md_ref, basis_ref,
+    local_hbm, anchor_hbm, momentum_hbm, ld_hbm, ad_hbm, md_hbm, basis_hbm,
     h_ref, x_ref, dg_ref, dw_ref, abuf, mbuf,
-    lbuf, eh, el, bas, dd, drecv, f2, frecv, fsum, xt_ref, m_ref, mrecv1, mrecv2, msum, mrecv3, mz,
+    ld_ref, ad_ref, md_ref, basis_ref, lbuf, eh, el, bas, dd, drecv, f2, frecv, fsum, xt_ref, m_ref, mrecv1, mrecv2, msum, mrecv3, mz,
     gsend, grecv, gz, gram,
-    lsem, asem, msem, ssem, rsem,
+    small_sem, lsem, asem, msem, ssem, rsem,
 ):
     rep = lax.axis_index("rep")
     shard = lax.axis_index("shard")
     z, core = shard // CORES, shard % CORES
     other = 1 - core
     width = lbuf.shape[2]
-    rank = basis_ref.shape[1]
+    rank = basis_ref.shape[0]
 
     def rep_dev(j):
         return ((rep + j) % GROUPS, shard)
@@ -88,6 +88,14 @@
         started.append(copy)
         return copy
 
+    small = [
+        pltpu.make_async_copy(src, dst, small_sem.at[i])
+        for i, (src, dst) in enumerate(
+            ((basis_hbm, basis_ref), (ld_hbm, ld_ref), (ad_hbm, ad_ref), (md_hbm, md_ref))
+        )
+    ]
+    for copy in small:
+        copy.start()
     differences = ((local_hbm, lbuf, lsem), (anchor_hbm, abuf, asem))
     momenta = ((momentum_hbm, mbuf, msem),)
 
@@ -109,7 +117,9 @@
     for dev in peers:
         pl.semaphore_signal(barrier, inc=1, device_id=dev, device_id_type=MESH)
 
-    b = basis_ref[...]
+    for copy in small:
+        copy.wait()
+    b = basis_ref[...].T
     b_hi = b.astype(bf16)
     b_lo = (b - b_hi.astype(f32)).astype(bf16)
     bas[shard] = jnp.concatenate([b_hi, b_lo], axis=1)
@@ -192,27 +202,34 @@
     gsend[...] = jnp.where(lane_g < rank, g[:fold], g[fold:])
     gram_core = send(gsend, grecv, core_dev)
 
+    def coefficient(k):
+        m = jnp.dot(xt_ref[...], eh[k], preferred_element_type=f32)
+        m += jnp.dot(xt_ref[...], el[k], preferred_element_type=f32)
+        m_ref[k] = m[:rank] + m[rank:]
+
+    @pl.loop(0, GROUPS)
+    def _(i):
+        coefficient(other * GROUPS + i)
+
+    coeff_core = send(m_ref.at[pl.ds(other * GROUPS, GROUPS)], mrecv1, core_dev)
+
+    @pl.loop(0, GROUPS)
+    def _(i):
+        coefficient(core * GROUPS + i)
+
+    gram_core.wait_recv()
+    gz[z] = gsend[...] + grecv[...]
+    gram_z = [send(gz.at[z], gz.at[z], z_dev(j)) for j in (1, 2, 3)]
+
+    coeff_core.wait_recv()
+    mrecv1[...] += m_ref[pl.ds(core * GROUPS, GROUPS)]
+    coeff_rs = [send(mrecv1.at[(rep + j) % GROUPS], mrecv2.at[j - 1], rep_dev(j)) for j in (1, 2, 3)]
+
     for copy in weights_z:
         copy.wait_recv()
     first, second = pl.ds(0, GROUPS // 2), pl.ds(GROUPS // 2, GROUPS // 2)
     ours = dw_ref.at[core, rep, first]
     weights_first = [send(ours, ours, rep_dev(j)) for j in (1, 2, 3)]
-
-    @pl.loop(0, CHUNKS)
-    def _(k):
-        m = jnp.dot(xt_ref[...], eh[k], preferred_element_type=f32)
-        m += jnp.dot(xt_ref[...], el[k], preferred_element_type=f32)
-        m_ref[k] = m[:rank] + m[rank:]
-
-    coeff_core = send(m_ref.at[pl.ds(other * GROUPS, GROUPS)], mrecv1, core_dev)
-    gram_core.wait_recv()
-    gz[z] = gsend[...] + grecv[...]
-    gram_z = [send(gz.at[z], gz.at[z], z_dev(j)) for j in (1, 2, 3)]
-
-    coeff_core.wait_recv()
-    mrecv1[...] += m_ref[pl.ds(core * GROUPS, GROUPS)]
-    coeff_rs = [send(mrecv1.at[(rep + j) % GROUPS], mrecv2.at[j - 1], rep_dev(j)) for j in (1, 2, 3)]
-
     ours = dw_ref.at[core, rep, second]
     weights_second = [send(ours, ours, rep_dev(j)) for j in (1, 2, 3)]
 
@@ -294,16 +311,13 @@
                   dn_out, dm_out, dw_out, new_out, mom_out, nbuf, pbuf, nsem, psem, wsem):
     rank = h_ref.shape[1] // 2
     width = h_ref.shape[2]
-    rows = x_ref.shape[0]
-    step = rows // 4
-
     def weights(at):
         return pltpu.make_async_copy(
             dw_ref.at[at % CORES, :, at // CORES], dw_out.at[at // CORES, at % CORES], wsem.at[at]
         )
 
     def out(k):
-        cols = pl.ds(k * width, width)
+        cols = pl.ds(pl.multiple_of(k * width, width), width)
         return (
             pltpu.make_async_copy(nbuf.at[k % 2], new_out.at[:, cols], nsem.at[k % 2]),
             pltpu.make_async_copy(pbuf.at[k % 2], mom_out.at[:, cols], psem.at[k % 2]),
@@ -311,22 +325,23 @@
 
     for at in range(CHUNKS):
         weights(at).start()
-    for k in range(CHUNKS):
+    x2 = jnp.concatenate([x_ref[...], x_ref[...]], axis=1)
+
+    @pl.loop(0, CHUNKS)
+    def _(k):
         hi, lo = h_ref[k, :rank, :], h_ref[k, rank:, :]
         right = jnp.concatenate([hi, hi, lo, lo], axis=0)
-        if k >= 2:
+
+        @pl.when(k >= 2)
+        def _():
             for copy in out(k - 2):
                 copy.wait()
 
-        @pl.loop(0, rows // step)
-        def _(t):
-            at = pl.ds(pl.multiple_of(t * step, step), step)
-            x = x_ref[at, :]
-            grad = jnp.dot(jnp.concatenate([x, x], axis=1), right, preferred_element_type=f32)
-            nbuf[k % 2, at, :], pbuf[k % 2, at, :] = nesterov(grad, anchor_ref[k, at, :], mom_ref[k, at, :])
-
+        grad = jnp.dot(x2, right, preferred_element_type=f32)
+        nbuf[k % 2], pbuf[k % 2] = nesterov(grad, anchor_ref[k], mom_ref[k])
         for copy in out(k):
             copy.start()
+
     dn_out[...], dm_out[...] = nesterov(dg_ref[...], ad_ref[...], md_ref[...])
     for k in (CHUNKS - 2, CHUNKS - 1):
         for copy in out(k):
@@ -347,6 +362,7 @@
     vmem = pl.BlockSpec(memory_space=pltpu.VMEM)
     hbm = pl.BlockSpec(memory_space=pltpu.HBM)
     S = jax.ShapeDtypeStruct
+    stay = lambda array: pltpu.with_memory_space_constraint(array, pltpu.HBM)
     h, x, dg, dw, anchor, momentum = pl.pallas_call(
         exchange_kernel,
         out_shape=(
@@ -357,9 +373,13 @@
             S((CHUNKS, rows, width), f32),
             S((CHUNKS, rows, width), f32),
         ),
-        in_specs=[hbm] * 3 + [vmem] * 4,
+        in_specs=[hbm] * 7,
         out_specs=(vmem,) * 6,
         scratch_shapes=[
+            pltpu.VMEM(quarters, f32),
+            pltpu.VMEM(quarters, f32),
+            pltpu.VMEM(quarters, f32),
+            pltpu.VMEM((rank, width), f32),
             pltpu.VMEM((CHUNKS, rows, width), f32),
             pltpu.VMEM((CHUNKS, rows, width), bf16),
             pltpu.VMEM((CHUNKS, rows, width), bf16),
@@ -380,6 +400,7 @@
             pltpu.VMEM((rank // 2, lanes), f32),
             pltpu.VMEM((GROUPS, rank // 2, lanes), f32),
             pltpu.VMEM((rank, lanes), f32),
+            pltpu.SemaphoreType.DMA((4,)),
             pltpu.SemaphoreType.DMA((CHUNKS,)),
             pltpu.SemaphoreType.DMA((CHUNKS,)),
             pltpu.SemaphoreType.DMA((CHUNKS,)),
@@ -390,8 +411,8 @@
             collective_id=0, has_side_effects=True, vmem_limit_bytes=LIMIT1
         ),
     )(
-        local_emb[0], anchor_emb, momentum_emb, local_dense[0].reshape(quarters), anchor_dense.reshape(quarters),
-        momentum_dense.reshape(quarters), proj_basis,
+        local_emb[0], anchor_emb, momentum_emb, stay(local_dense[0].reshape(quarters)),
+        stay(anchor_dense.reshape(quarters)), stay(momentum_dense.reshape(quarters)), stay(proj_basis.T),
     )
 
     dn, dm, weights, new, mom = pl.pallas_call(

time: 71.2 us -> 61.8 us (0.87)
  Pallas kernels: 66.2 us -> 61 us
  local copies, waits for them, and re-layouts: 4.06 us -> 0.01 us
    unnamed x11 -> x4, local copies, waits for them, and re-layouts: 4.06 us -> 0.01 us
    pallas_call x1, Pallas kernels: 55.6 us -> 52.1 us  [fused(): pl.pallas_call(exchange_kernel, out_shape=(S((CHUNKS, lanes, width), bf16...]
    pallas_call x1, Pallas kernels: 10.6 us -> 8.83 us  [fused(): pl.pallas_call(update_kernel, out_shape=(S(anchor_dense.shape, f32), S(an...]
where the time goes in v3:
time: 61.8 us; the launch traced here: 61.6 us
  Pallas kernels  61 us (99%)
  between operations  0.67 us (1%)
    pallas_call x1, Pallas kernels, fused(): pl.pallas_call(exchange_kernel, out_shape=(S((CHUNKS, lanes, width), bf16...  52.1 us
    pallas_call x1, Pallas kernels, fused(): pl.pallas_call(update_kernel, out_shape=(S(anchor_dense.shape, f32), S(an...  8.83 us

profile of v3, /device:TPU:0, one launch (start us, length us, event | category | flops | bytes accessed | tf_op | source)
XLA Modules:
  0.0 61.6 jit_solution(7632545889243145854)
XLA Ops:
  0.6 0.0 copy-start
  0.6 0.0 copy-start.1
  0.7 52.1 %shard_map.110 = (bf16[8,128,256]{2,1,0:T(8,128)(2,1)S(1)}, bf16[1024,128]{1,0:T(8,128)(2,1)S(1)}, f32[4,32,1024]{2,1,0:T(8,128)S(1)}, bf16[2,4,4,32,1024]{4,3,2...) custom-call(f32[1024,2048]{1,0:T(8,128)} %bitcast.10, f32[1024,2048]{1,0:T(8,128)} %anchor_hbm.1, ...), custom_call_target="tpu_custom_call" | custom-call | tf_op jit(solution)/shard_map/pallas_call | solution.py:366
  52.8 0.0 copy-done
  52.8 0.0 copy-done.1
  52.8 8.8 %shard_map.111 = (f32[128,1024]{1,0:T(8,128)}, f32[128,1024]{1,0:T(8,128)}, bf16[4,2,4,32,1024]{4,3,2,1,0:T(8,128)(2,1)}, f32[1024,2048]{1,0:T(8,128)}, f32[1024,2048]{1,0:T(8,128)}) custom-call(bf16[1024,128]{1,0:T(8,128)(2,1)S(1)} %get-tuple-element.16.x_ref, bf16[8,128,256]{2,1,0:T(8,128)(2,1)S(1)} %get-tuple-element.17.h_ref, ...), custom_call_target="tpu_custom_call" | custom-call | tf_op jit(solution)/shard_map/pallas_call | solution.py:418
Async XLA Ops:
  0.6 52.2 %copy-start = (f32[128,1024]{1,0:T(8,128)S(1)}, f32[128,1024]{1,0:T(8,128)}, u32[]{:S(2)}) copy-start(f32[128,1024]{1,0:T(8,128)} %ad_ref.1) | copy-start | bytes 1572868
  0.6 52.2 %copy-start.1 = (f32[128,1024]{1,0:T(8,128)S(1)}, f32[128,1024]{1,0:T(8,128)}, u32[]{:S(2)}) copy-start(f32[128,1024]{1,0:T(8,128)} %md_ref.1) | copy-start | bytes 1572868
